TPU v7x, 512 devices: a whole 4x4x16 slice. The times are simulated.
512 devices in a mesh: seq: 64 (over y_hi, z, core), tp: 8 (over x, y_lo).
Axes of the slice: x: 4, y: 4 (y_hi: 2, y_lo: 2; y = y_hi * 2 + y_lo), z: 16, core: 2. Of those that a mesh axis runs over, the one named last changes fastest.
Arguments:
- queries: bfloat16 [65536, 4096], P('seq', 'tp'), may hold values from -600 to 600
- neighbours: bfloat16 [512, 896, 128], P('seq', 'tp'), may hold values from -6 to 6
- key_weight: bfloat16 [896, 4096], P(None, 'tp'), may hold values from -0.1875 to 0.1875
- value_weight: bfloat16 [896, 4096], P(None, 'tp'), may hold values from -0.1875 to 0.1875
- neighbour_ids: int32 [1024, 2], P('seq'), may hold values from 0 to 511, as said below
Outputs:
- attended: bfloat16 [65536, 4096], P('seq', 'tp')
Inputs may be any that keep to these rules, and one draw needn't show every extreme that they name: `neighbour_ids`: block b is stored on index b // 8 of seq. Among the 32 neighbours of the spans of one index of seq, at most 1 are stored on any one index of seq, and exactly 1 on some.
All inputs are finite; a program needn't handle non-finite values.
Results may differ from a plain program's by a relative error of at most 0.014.
Values may be sent and summed in bfloat16 or wider, within the bound.
A program may use at most 64 MiB of HBM per device.

v0:
```python
import jax
import jax.numpy as jnp
from jax import lax
from jax.sharding import PartitionSpec as P

HDIM = 128
SPAN = 64


def passed_along(x, axis, by):
    peers = lax.axis_size(axis)
    pairs = [(i, i + by) for i in range(peers) if 0 <= i + by < peers]
    return lax.ppermute(x, axis, pairs)


def slot_ranks(sources):
    positions = sources.shape[-1]
    alike = sources[..., :, None] == sources[..., None, :]
    earlier = jnp.arange(positions)[None, :] < jnp.arange(positions)[:, None]
    return jnp.sum(jnp.where(alike & earlier, 1, 0), axis=-1).astype(jnp.int32)


def partial_attention(query_rows, key_rows, value_rows, head_count):
    groups = query_rows.shape[0]
    columns = query_rows.shape[-1]
    head_dim = columns // head_count
    query_heads = query_rows.reshape(groups, -1, head_count, head_dim)
    key_heads = key_rows.reshape(groups, -1, head_count, head_dim)
    value_heads = value_rows.reshape(groups, -1, head_count, head_dim)
    scores = jnp.einsum(
        "gqhd,gkhd->ghqk", query_heads, key_heads, preferred_element_type=jnp.float32
    ) * head_dim ** (-0.5)
    highest = jnp.max(scores, axis=-1, keepdims=True)
    exponent = jnp.exp(scores - highest)
    totals = jnp.sum(exponent, axis=-1, keepdims=True)
    weights = (exponent / totals).astype(jnp.bfloat16)
    blended = jnp.einsum(
        "ghqk,gkhd->gqhd", weights, value_heads, preferred_element_type=jnp.float32
    )
    log_totals = (highest + jnp.log(totals))[..., 0]
    return (blended.astype(jnp.bfloat16).reshape(groups, -1, columns), log_totals)


def combine_pair(partials, log_totals, head_count):
    largest = jnp.max(log_totals, axis=1, keepdims=True)
    shares = jnp.exp(log_totals - largest)
    shares = shares / jnp.sum(shares, axis=1, keepdims=True)
    shares = jnp.transpose(shares, (0, 1, 3, 2))[..., None]
    span_count, _, window_rows, columns = partials.shape
    spread = partials.reshape(span_count, 2, window_rows, head_count, columns // head_count).astype(
        jnp.float32
    )
    return (
        jnp.sum(shares * spread, axis=1)
        .reshape(span_count, window_rows, columns)
        .astype(jnp.bfloat16)
    )


def shards(queries, neighbours, key_weight, value_weight, neighbour_ids):
    tok_rows, columns = queries.shape
    head_count = columns // HDIM
    span_count = neighbour_ids.shape[0]
    seq_count = lax.axis_size("seq")
    block_count = neighbours.shape[0]
    slots_per = (2 * span_count + seq_count - 1) // seq_count
    edge_rows = SPAN - 1
    incoming = passed_along(queries[:edge_rows], "seq", -1)
    windows = jnp.concatenate([queries[edge_rows:], incoming], axis=0).reshape(
        span_count, SPAN, columns
    )
    all_ids = lax.all_gather(neighbour_ids, "seq", axis=0, tiled=True).reshape(
        seq_count, 2 * span_count
    )
    own_index = lax.axis_index("seq")
    all_sources = all_ids // block_count
    all_ranks = slot_ranks(all_sources)
    own_ids = neighbour_ids.reshape(2 * span_count)
    own_sources = own_ids // block_count
    own_ranks = slot_ranks(own_sources)
    slot_grid = jnp.arange(slots_per)
    matches = (all_sources[:, :, None] == own_index) & (
        all_ranks[:, :, None] == slot_grid[None, None, :]
    )
    stored = jnp.sum(jnp.where(matches, (all_ids % block_count)[:, :, None], 0), axis=1)
    picked = (own_sources[None, None, :] == jnp.arange(seq_count)[:, None, None]) & (
        own_ranks[None, None, :] == slot_grid[None, :, None]
    )
    picked = jnp.sum(
        picked.reshape(seq_count, slots_per, span_count, 2).astype(jnp.float32), axis=-1
    ).astype(jnp.bfloat16)
    outgoing = jnp.einsum(
        "scu,uqw->scqw", picked, windows, preferred_element_type=jnp.float32
    ).astype(jnp.bfloat16)
    arrived = lax.all_to_all(outgoing, "seq", split_axis=0, concat_axis=0, tiled=True)
    segment = lax.all_gather(neighbours, "tp", axis=1, tiled=True)
    key_sums = jnp.einsum("bfr,fk->brk", segment, key_weight, preferred_element_type=jnp.float32)
    value_sums = jnp.einsum(
        "bfr,fk->brk", segment, value_weight, preferred_element_type=jnp.float32
    )
    key_rows = key_sums.astype(jnp.bfloat16)
    value_rows = value_sums.astype(jnp.bfloat16)
    total_slots = seq_count * slots_per
    group_size = 8
    slot_queries = arrived.reshape(total_slots // group_size, group_size, SPAN, columns)
    slot_blocks = stored.reshape(total_slots // group_size, group_size)

    def attend(operands):
        query_group, block_group = operands
        return partial_attention(
            query_group, key_rows[block_group], value_rows[block_group], head_count
        )

    partials, log_totals = lax.map(attend, (slot_queries, slot_blocks))
    partials = partials.reshape(seq_count, slots_per, SPAN, columns)
    log_totals = log_totals.reshape(seq_count, slots_per, head_count, SPAN)
    returned = lax.all_to_all(partials, "seq", split_axis=0, concat_axis=0, tiled=True)
    returned_totals = lax.all_to_all(log_totals, "seq", split_axis=0, concat_axis=0, tiled=True)
    pair_parts = returned[own_sources, own_ranks].reshape(span_count, 2, SPAN, columns)
    pair_totals = returned_totals[own_sources, own_ranks].reshape(span_count, 2, head_count, SPAN)
    blended = combine_pair(pair_parts, pair_totals, head_count).reshape(span_count * SPAN, columns)
    carried = passed_along(blended[tok_rows - edge_rows :], "seq", 1)
    return jnp.concatenate([carried, blended[: tok_rows - edge_rows]], axis=0)


def solution(mesh):
    in_specs = (P("seq", "tp"), P("seq", "tp", None), P(None, "tp"), P(None, "tp"), P("seq", None))
    out_specs = P("seq", "tp")
    return jax.shard_map(shards, mesh=mesh, in_specs=in_specs, out_specs=out_specs, check_vma=False)
```

profile of v0, /device:TPU:1, one launch (start us, length us, event | category | flops | bytes accessed | tf_op | source)
XLA Modules:
  0.0 622.7 jit_solution(8957665849714258802)
XLA Ops:
  7.5 8.8 %collective-permute-start = (bf16[63,512]{1,0:T(8,128)(2,1)S(1)}, bf16[63,512]{1,0:T(8,128)(2,1)S(1)}, u32[]{:S(2)}, u32[]{:S(2)}) collective-permute-start(bf16[63,512]{1,0:T(8,128)(2,1)S(1)} %slice.13), channel_id=1, source_target_pairs={{8,0},{16,8},{24,16},{32,24},{40,32},{48,40},{56,48},{64,56},{72,6... | collective-permute-start | bytes 193544 | tf_op jit(solution)/shard_map/ppermute | solution.py:13
  17.7 1.4 slice.12
  21.6 4.4 copy.56
  26.0 13.3 %all-to-all-start = ((bf16[64,1,64,512]{3,2,1,0:T(8,128)(2,1)}), bf16[64,1,64,512]{3,2,1,0:T(8,128)(2,1)}, u32[]{:S(2)}, u32[]{:S(2)}) async-start(bf16[64,1,64,512]{3,2,1,0:T(8,128)(2,1)} %copy.56), calls=%async_computation | async-start | bytes 8388608 | tf_op jit(solution)/shard_map/all_to_all | solution.py:95
  40.1 247.8 %all-gather = s32[64,16,2]{1,2,0:T(2,128)S(1)} all-gather(s32[1,16,2]{1,2,0:T(2,128)S(1)} %bitcast.96), channel_id=1, replica_groups=mesh['seq'=64,'tp'=8] {'seq'}, dimensions={0}, use_global_device_ids=true | all-gather | bytes 8320 | tf_op jit(solution)/shard_map/all_gather | solution.py:72
  290.1 2.8 convolution_convert_fusion.1
  292.8 3.8 convolution_convert_fusion.2
  296.6 89.0 %while.12 = (s32[]{:T(128)}, bf16[8,8,64,512]{3,2,1,0:T(8,128)(2,1)}, f32[8,8,4,64]{3,2,1,0:T(4,128)}, s32[8,8]{1,0:T(8,128)}, bf16[8,128,512]{2,1,0:T(8,128)(2,...) while((s32[]{:T(128)}, bf16[8,8,64,512]{3,2,1,0:T(8,128)(2,1)}, ...), condition=%wide.region_8.9_spmd, body=%wide.region_5.8_spmd.sunk | while | flops 136313888 | bytes 15806733 | solution.py:114
  298.5 2.9 gather_fusion.1
  303.6 2.0 fusion.46
  309.6 2.9 gather_fusion.1
  314.8 2.0 fusion.46
  320.8 2.9 gather_fusion.1
  325.9 2.0 fusion.46
  331.9 2.9 gather_fusion.1
  337.0 2.0 fusion.46
  343.0 2.9 gather_fusion.1
  348.2 2.0 fusion.46
  354.2 2.9 gather_fusion.1
  359.3 2.0 fusion.46
  365.3 2.9 gather_fusion.1
  370.4 2.0 fusion.46
  376.4 2.9 gather_fusion.1
  381.5 2.0 fusion.46
  386.7 19.8 %all_to_all.15 = f32[64,1,256]{2,1,0:T(1,128)S(1)} all-to-all(f32[64,1,256]{2,1,0:T(1,128)S(1)} %reshape.437), channel_id=1, replica_groups=mesh['seq'=64,'tp'=8] {'seq'}, dimensions={0} | all-to-all | bytes 131072 | tf_op jit(solution)/shard_map/all_to_all | solution.py:118
  406.5 5.5 all-to-all-start.2
  415.7 181.6 %all-to-all-done.2 = bf16[64,1,64,512]{3,2,1,0:T(8,128)(2,1)} async-done(((bf16[64,1,64,512]{3,2,1,0:T(8,128)(2,1)}), bf16[64,1,64,512]{3,2,1,0:T(8,128)(2,1)}, u32[]{:S(2)}, u32[]{:S(2)}) %all-to-all-start.2) | async-done | bytes 4194336 | tf_op jit(solution)/shard_map/all_to_all | solution.py:117
  597.4 2.9 gather_fusion.3
  600.2 3.0 reshape.402
  603.3 5.1 multiply_reduce_fusion
  608.6 2.2 collective-permute-start.1
  610.9 3.8 collective-permute-done.1
  (150 shorter events, 63.3 us)
Async XLA Ops:
  6.5 283.5 %copy-start = (bf16[896,512]{1,0:T(8,128)(2,1)S(1)}, bf16[896,512]{1,0:T(8,128)(2,1)}, u32[]{:S(2)}) copy-start(bf16[896,512]{1,0:T(8,128)(2,1)} %param.9) | copy-start | bytes 2752516
  7.5 12.8 %collective-permute-start = (bf16[63,512]{1,0:T(8,128)(2,1)S(1)}, bf16[63,512]{1,0:T(8,128)(2,1)S(1)}, u32[]{:S(2)}, u32[]{:S(2)}) collective-permute-start(bf16[63,512]{1,0:T(8,128)(2,1)S(1)} %slice.13), channel_id=1, source_target_pairs={{8,0},{16,8},{24,16},{32,24},{40,32},{48,40},{56,48},{64,56},{72,6... | collective-permute-start | bytes 193544 | tf_op jit(solution)/shard_map/ppermute | solution.py:13
  17.7 3.9 copy-start.2
  19.4 0.6 copy-start.5
  26.0 14.1 %copy-start.4 = (s32[16,2]{0,1:T(2,128)S(1)}, s32[16,2]{0,1:T(2,128)}, u32[]{:S(2)}) copy-start(s32[16,2]{0,1:T(2,128)} %param.11) | copy-start | bytes 388
  26.0 270.6 %all-to-all-start = ((bf16[64,1,64,512]{3,2,1,0:T(8,128)(2,1)}), bf16[64,1,64,512]{3,2,1,0:T(8,128)(2,1)}, u32[]{:S(2)}, u32[]{:S(2)}) async-start(bf16[64,1,64,512]{3,2,1,0:T(8,128)(2,1)} %copy.56), calls=%async_computation | async-start | bytes 8388608 | tf_op jit(solution)/shard_map/all_to_all | solution.py:95
  39.4 253.5 %copy-start.1 = (bf16[896,512]{1,0:T(8,128)(2,1)S(1)}, bf16[896,512]{1,0:T(8,128)(2,1)}, u32[]{:S(2)}) copy-start(bf16[896,512]{1,0:T(8,128)(2,1)} %param.10) | copy-start | bytes 2752516
  39.4 250.7 %all-gather.3.cloned.1.call-start = ((), (), s32[]{:S(2)}) async-start(), calls=%async_computation.3 | async-start | bytes 2064384 | tf_op jit(solution)/shard_map/all_gather | solution.py:96
  406.5 5.6 copy-start.3
  406.5 5.7 copy-start.6
  406.5 190.9 %all-to-all-start.2 = ((bf16[64,1,64,512]{3,2,1,0:T(8,128)(2,1)}), bf16[64,1,64,512]{3,2,1,0:T(8,128)(2,1)}, u32[]{:S(2)}, u32[]{:S(2)}) async-start(bf16[64,1,64,512]{3,2,1,0:T(8,128)(2,1)} %bitcast.91), calls=%async_computation.2 | async-start | bytes 8388608 | tf_op jit(solution)/shard_map/all_to_all | solution.py:117
  608.6 6.1 collective-permute-start.1
Sparse Core Ops, SparseCore 0:
  42.3 59.5 all-gather.2
where the time goes:
time: 630 us; the launch traced here: 623 us
  blocking collectives  268 us (43%)
  waiting for transfers between devices  186 us (30%)
  local copies, waits for them, and re-layouts  69.5 us (11%)
  matrix products  30.8 us (5%)
  starting transfers between devices  29.9 us (5%)
  other arithmetic  24.6 us (4%)
  between operations  13.7 us (2%)
    all_gather x1, blocking collectives, shards(): lax.all_gather(neighbour_ids, 'seq', axis=0, tiled=True)  248 us
    all_to_all x1, waiting for transfers between devices, shards(): lax.all_to_all(partials, 'seq', split_axis=0, concat_axis=0, tiled=True)  182 us
    gather x8, local copies, waits for them, and re-layouts, attend(): value_rows[block_group]  23.3 us
    all_to_all x1, blocking collectives, shards(): lax.all_to_all(log_totals, 'seq', split_axis=0, concat_axis=0, tiled=True)  19.8 us
    dot_general x8, matrix products, partial_attention(): jnp.einsum('ghqk,gkhd->gqhd', weights, value_heads, preferred_element_typ...  15.7 us
    all_to_all x1, starting transfers between devices, shards(): lax.all_to_all(outgoing, 'seq', split_axis=0, concat_axis=0, tiled=True)  13.3 us
  transfers between devices with their start and end apart: 5, of which 2 were waited for; matrix products, arithmetic and copies ran while one was open for 3% of the time, Pallas kernels for 0%

commit v1 on v0

v1 whole, which is shorter than its diff:
```python
import jax
import jax.numpy as jnp
from jax import lax
from jax.experimental import pallas as pl
from jax.experimental.pallas import tpu as pltpu
from jax.sharding import PartitionSpec as P

HDIM = 128
SPAN = 64


def passed_along(x, axis, by):
    peers = lax.axis_size(axis)
    pairs = [(i, i + by) for i in range(peers) if 0 <= i + by < peers]
    return lax.ppermute(x, axis, pairs)


def attend_kernel(w_ref, x_ref, q_ref, o_ref):
    features = jnp.concatenate([x_ref[0], x_ref[1]], axis=1)
    rows = jnp.dot(w_ref[...], features, preferred_element_type=jnp.float32).astype(jnp.bfloat16)
    columns = q_ref.shape[1]
    for head in range(columns // HDIM):
        at = head * HDIM
        scores = jnp.dot(
            q_ref[:, at : at + HDIM], rows[at : at + HDIM], preferred_element_type=jnp.float32
        ) * (HDIM**-0.5)
        highest = jnp.max(scores, axis=1, keepdims=True)
        exponent = jnp.exp(scores - highest)
        totals = jnp.sum(exponent, axis=1, keepdims=True)
        blended = lax.dot_general(
            exponent.astype(jnp.bfloat16),
            rows[columns + at : columns + at + HDIM],
            (((1,), (1,)), ((), ())),
            preferred_element_type=jnp.float32,
        )
        o_ref[:, at : at + HDIM] = (blended / totals).astype(jnp.bfloat16)


def shards(queries, neighbours, key_weight, value_weight, neighbour_ids):
    tok_rows, columns = queries.shape
    span_count = neighbour_ids.shape[0]
    edge_rows = SPAN - 1
    incoming = passed_along(queries[:edge_rows], "seq", -1)
    windows = jnp.concatenate([queries[edge_rows:], incoming], axis=0)
    stored = lax.all_gather(neighbours, "seq", axis=0, tiled=True)
    chosen = stored[neighbour_ids.reshape(-1)]
    features = lax.all_gather(chosen, "tp", axis=1, tiled=True)
    weights = jnp.concatenate([key_weight, value_weight], axis=1).T
    depth = weights.shape[1]
    blended = pl.pallas_call(
        attend_kernel,
        out_shape=jax.ShapeDtypeStruct((tok_rows, columns), jnp.bfloat16),
        grid=(span_count,),
        in_specs=[
            pl.BlockSpec((2 * columns, depth), lambda i: (0, 0)),
            pl.BlockSpec((2, depth, features.shape[2]), lambda i: (i, 0, 0)),
            pl.BlockSpec((SPAN, columns), lambda i: (i, 0)),
        ],
        out_specs=pl.BlockSpec((SPAN, columns), lambda i: (i, 0)),
        compiler_params=pltpu.CompilerParams(vmem_limit_bytes=40 * 1024 * 1024),
    )(weights, features, windows)
    carried = passed_along(blended[tok_rows - edge_rows :], "seq", 1)
    return jnp.concatenate([carried, blended[: tok_rows - edge_rows]], axis=0)


def solution(mesh):
    in_specs = (P("seq", "tp"), P("seq", "tp", None), P(None, "tp"), P(None, "tp"), P("seq", None))
    out_specs = P("seq", "tp")
    return jax.shard_map(shards, mesh=mesh, in_specs=in_specs, out_specs=out_specs, check_vma=False)
```

time: 630 us -> 409 us (0.65)
  blocking collectives: 268 us -> 0 us
  waiting for transfers between devices: 186 us -> 342 us
  local copies, waits for them, and re-layouts: 69.5 us -> 13.9 us
  matrix products: 30.8 us -> 0 us
  Pallas kernels: 0 us -> 25.3 us
  starting transfers between devices: 29.9 us -> 5.94 us
  other arithmetic: 24.6 us -> 2.72 us
    all_gather x1 -> x2, waiting for transfers between devices: 0.01 us -> 340 us  [the longest x1 196 us: shards(): stored = lax.all_gather(neighbours, 'seq', axis=0, tiled=True)]
    all_gather x1 -> x0, blocking collectives: 248 us -> none  [shards(): lax.all_gather(neighbour_ids, 'seq', axis=0, tiled=True)]
    all_to_all x2 -> x0, waiting for transfers between devices: 182 us -> none  [the longest x1 182 us: shards(): lax.all_to_all(partials, 'seq', split_axis=0, concat_axis=0, tiled=True)]
    dot_general x19 -> x0, matrix products: 30.8 us -> none  [the longest x8 15.7 us: partial_attention(): jnp.einsum('ghqk,gkhd->gqhd', weights, value_heads, preferred_element_typ...]
    pallas_call x0 -> x1, Pallas kernels: none -> 25.3 us  [shards(): pl.pallas_call(attend_kernel, out_shape=jax.ShapeDtypeStruct((tok_rows, c...]
    gather x18 -> x1, local copies, waits for them, and re-layouts: 31.6 us -> 6.79 us  [shards(): chosen = stored[neighbour_ids.reshape(-1)]]
    all_to_all x1 -> x0, blocking collectives: 19.8 us -> none  [shards(): lax.all_to_all(log_totals, 'seq', split_axis=0, concat_axis=0, tiled=True)]
    all_to_all x2 -> x0, starting transfers between devices: 18.9 us -> none  [the longest x1 13.3 us: shards(): lax.all_to_all(outgoing, 'seq', split_axis=0, concat_axis=0, tiled=True)]
  transfers between devices with their start and end apart: 5 -> 4, of which waited for: 2 -> 3; matrix products, arithmetic and copies ran while one was open for 3% -> 1% of each run, Pallas kernels for 0% -> 0%
where the time goes in v1:
time: 409 us; the launch traced here: 404 us
  waiting for transfers between devices  342 us (84%)
  Pallas kernels  25.3 us (6%)
  local copies, waits for them, and re-layouts  13.9 us (3%)
  between operations  13.5 us (3%)
  starting transfers between devices  5.94 us (1%)
    all_gather x1, waiting for transfers between devices, shards(): stored = lax.all_gather(neighbours, 'seq', axis=0, tiled=True)  196 us
    all_gather x1, waiting for transfers between devices, shards(): features = lax.all_gather(chosen, 'tp', axis=1, tiled=True)  145 us
    pallas_call x1, Pallas kernels, shards(): pl.pallas_call(attend_kernel, out_shape=jax.ShapeDtypeStruct((tok_rows, c...  25.3 us
  transfers between devices with their start and end apart: 4, of which 3 were waited for; matrix products, arithmetic and copies ran while one was open for 1% of the time, Pallas kernels for 0%

profile of v1, /device:TPU:1, one launch (start us, length us, event | category | flops | bytes accessed | tf_op | source)
XLA Modules:
  0.0 403.7 jit_solution(11505327660882653479)
XLA Ops:
  6.5 0.0 copy-start.2
  6.5 0.0 all-gather.4.cloned.1.call-start
  6.5 0.7 all-gather.4.cloned.1.call-update
  7.3 0.0 all-gather.6.cloned.1.call-start
  7.3 0.8 copy.14
  8.1 0.1 reshape.31
  8.2 0.0 copy-start.3
  8.2 195.8 %all-gather.4.cloned.1.call-done = bf16[512,112,128]{2,1,0:T(8,128)(2,1)} async-done(((bf16[8,112,128]{2,1,0:T(8,128)(2,1)}), bf16[512,112,128]{2,1,0:T(8,128)(2,1)}) %all-gather.4.cloned.1.call-update) | async-done | bytes 14680080 | tf_op jit(solution)/shard_map/all_gather | solution.py:45
  204.0 6.8 %gather_fusion = bf16[32,112,128]{2,1,0:T(8,128)(2,1)} fusion(bf16[512,112,128]{2,1,0:T(8,128)(2,1)} %all-gather.4.cloned.1.call-done, s32[1024]{0:T(1024)S(1)} %pad_clamp_fusion), kind=kCustom, calls=%fused_computation | custom fusion | bytes 1835136 | tf_op jit(solution)/shard_map/gather | solution.py:46
  210.8 0.0 all-gather.6.cloned.1.call-update
  210.8 0.8 slice.13
  211.7 2.1 collective-permute-start
  213.8 0.0 copy-done.2
  213.8 0.6 copy.12
  214.4 0.0 copy-done.3
  214.4 1.3 copy.13
  215.7 0.0 copy-start.1
  215.7 1.4 maximum_bitcast_fusion.w_ref
  217.1 0.1 copy-done.1
  217.2 0.2 slice.12
  217.5 0.0 collective-permute-done
  217.5 0.1 pad_maximum_fusion.q_ref
  217.6 144.6 %all-gather.6.cloned.1.call-done.x_ref = bf16[32,896,128]{2,1,0:T(8,128)(2,1)} async-done(((bf16[32,112,128]{2,1,0:T(8,128)(2,1)}), bf16[32,896,128]{2,1,0:T(8,128)(2,1)}) %all-gather.6.cloned.1.call-update) | async-done | bytes 7340048 | tf_op jit(solution)/shard_map/all_gather | solution.py:47
  362.2 0.0 copy-start
  362.2 3.1 copy-done
  365.3 25.3 %shard_map.55 = bf16[1024,512]{1,0:T(8,128)(2,1)S(1)} custom-call(bf16[1024,896]{1,0:T(8,128)(2,1)S(1)} %maximum_bitcast_fusion.w_ref, bf16[32,896,128]{2,1,0:T(8,128)(2,1)S(1)} %copy-done, bf16[1024,512]{1,0:T(8,128)(2,1)S(1)} %pad_maximum_fusion.q_ref), custom_call_target="tpu_custom_call" | custom-call | tf_op jit(solution)/shard_map/pallas_call | solution.py:50
  390.6 3.7 collective-permute-start.1
  394.4 0.1 slice.19
  394.5 1.2 collective-permute-done.1
  395.7 1.2 pad_maximum_fusion.1
  (3 shorter events, 0.0 us)
Async XLA Ops:
  6.5 207.3 %copy-start.2 = (bf16[896,512]{1,0:T(8,128)(2,1)S(1)}, bf16[896,512]{1,0:T(8,128)(2,1)}, u32[]{:S(2)}) copy-start(bf16[896,512]{1,0:T(8,128)(2,1)} %param.7) | copy-start | bytes 2752516
  6.5 197.5 %all-gather.4.cloned.1.call-start = ((), (), s32[]{:S(2)}) async-start(), calls=%async_computation | async-start | bytes 14909440 | tf_op jit(solution)/shard_map/all_gather | solution.py:45
  7.3 354.9 %all-gather.6.cloned.1.call-start = ((), (), s32[]{:S(2)}) async-start(), calls=%async_computation.1 | async-start | bytes 8257536 | tf_op jit(solution)/shard_map/all_gather | solution.py:47
  8.2 206.3 %copy-start.3 = (bf16[896,512]{1,0:T(8,128)(2,1)S(1)}, bf16[896,512]{1,0:T(8,128)(2,1)}, u32[]{:S(2)}) copy-start(bf16[896,512]{1,0:T(8,128)(2,1)} %param.8) | copy-start | bytes 2752516
  211.7 5.8 %collective-permute-start = (bf16[63,512]{1,0:T(8,128)(2,1)S(1)}, bf16[63,512]{1,0:T(8,128)(2,1)S(1)}, u32[]{:S(2)}, u32[]{:S(2)}) collective-permute-start(bf16[63,512]{1,0:T(8,128)(2,1)S(1)} %slice.13), channel_id=1, source_target_pairs={{8,0},{16,8},{24,16},{32,24},{40,32},{48,40},{56,48},{64,56},{72,6... | collective-permute-start | bytes 193544 | tf_op jit(solution)/shard_map/ppermute | solution.py:15
  215.7 1.5 copy-start.1
  362.2 3.1 copy-start
  390.6 5.1 %collective-permute-start.1 = (bf16[63,512]{1,0:T(8,128)(2,1)S(1)}, bf16[63,512]{1,0:T(8,128)(2,1)S(1)}, u32[]{:S(2)}, u32[]{:S(2)}) collective-permute-start(bf16[63,512]{1,0:T(8,128)(2,1)S(1)} %slice.18), channel_id=1, source_target_pairs={{0,8},{8,16},{16,24},{24,32},{32,40},{40,48},{48,56},{56,64},{64,7... | collective-permute-start | bytes 193544 | tf_op jit(solution)/shard_map/ppermute | solution.py:15
Sparse Core Ops, SparseCore 0:
  10.6 193.3 all-gather.3
  210.9 151.1 all-gather.5

commit v2 on v1

v2 whole, which is shorter than its diff:
```python
import functools

import jax
import jax.numpy as jnp
from jax import lax
from jax.experimental import pallas as pl
from jax.experimental.pallas import tpu as pltpu
from jax.sharding import PartitionSpec as P

HDIM = 128
SPAN = 64
ZS = 16
XS = 4
CHUNKS = (32, 32, 48)
LAGS = (0, 6, 12)
MESH = pl.DeviceIdType.MESH


def passed_along(x, axis, by):
    peers = lax.axis_size(axis)
    pairs = [(i, i + by) for i in range(peers) if 0 <= i + by < peers]
    return lax.ppermute(x, axis, pairs)


def heads_of_span(weights, features, queries, head_count):
    rows = sum(
        jnp.dot(w, f, preferred_element_type=jnp.float32) for w, f in zip(weights, features)
    ).astype(jnp.bfloat16)
    columns = head_count * HDIM
    results = []
    for head in range(head_count):
        at = head * HDIM
        scores = jnp.dot(
            queries[:, at : at + HDIM], rows[at : at + HDIM], preferred_element_type=jnp.float32
        ) * (HDIM**-0.5)
        highest = jnp.max(scores, axis=1, keepdims=True)
        exponent = jnp.exp(scores - highest)
        totals = jnp.sum(exponent, axis=1, keepdims=True)
        blended = lax.dot_general(
            exponent.astype(jnp.bfloat16),
            rows[columns + at : columns + at + HDIM],
            (((1,), (1,)), ((), ())),
            preferred_element_type=jnp.float32,
        )
        results.append((blended / totals).astype(jnp.bfloat16))
    return jnp.concatenate(results, axis=1)


def ring_events(chunks):
    events = []
    for q in range(chunks):
        for step in range(1, ZS // 2 + 1):
            events.append((LAGS[q] + step, 0, ("ring", q, step)))
        done = LAGS[q] + ZS // 2
        events.append((done, 1, ("pick", q)))
        events.append((done + 3, 2, ("sort", q)))
    return [what for _, _, what in sorted(events)]


def kernel(
    ids_ref, table_ref, stored_ref, weight_ref, window_ref, out_ref, *scratch, n_chunks, head_count
):
    n = n_chunks
    gathered, picked, slots, sorted_, features = (scratch[i * n : (i + 1) * n] for i in range(5))
    (weights, queries, results, tables, table_smem, send_sems, recv_sems, local_sems, back_send, back_recv) = (
        scratch[5 * n :]
    )
    s, t = lax.axis_index("seq"), lax.axis_index("tp")
    h, z, c = s // (2 * ZS), (s // 2) % ZS, s % 2
    x, l = t // 2, t % 2
    columns = head_count * HDIM
    spans = out_ref.shape[0] // SPAN
    mine = spans // XS
    counter = [0, 0]
    sent = []

    def at_seq(h_, z_, c_):
        return (h_ * (2 * ZS) + z_ * 2 + c_, t)

    def at_tp(x_, l_):
        return (s, x_ * 2 + l_)

    def send(src, dst, device):
        i = counter[0]
        counter[0] += 1
        copy = pltpu.make_async_remote_copy(
            src_ref=src,
            dst_ref=dst,
            send_sem=send_sems.at[i],
            recv_sem=recv_sems.at[i],
            device_id=device,
            device_id_type=MESH,
        )
        copy.start()
        sent.append(copy)
        return copy

    def local(src, dst):
        i = counter[1]
        counter[1] += 1
        copy = pltpu.make_async_copy(src, dst, local_sems.at[i])
        copy.start()
        return copy

    right, left = at_seq(h, (z + 1) % ZS, c), at_seq(h, (z + ZS - 1) % ZS, c)
    sides = [(0, 1), (1, 0), (1, 1)]
    side_devices = [at_seq((h + a) % 2, z, (c + b) % 2) for a, b in sides]
    x_of = [(x + d) % XS for d in range(XS)]
    other_core = side_devices[0]

    own_stored = []
    first = 0
    for q in range(n):
        count = CHUNKS[q]
        own_stored.append(local(stored_ref.at[:, pl.ds(first, count), :], gathered[q].at[z]))
        first += count
    own_weight = local(weight_ref, weights.at[x])
    own_table = local(table_ref, table_smem.at[0])

    barrier = pltpu.get_barrier_semaphore()
    partners = [right, left] + side_devices
    partners += [at_tp(x_of[d], (l + e) % 2) for d in range(XS) for e in range(2) if (d, e) != (0, 0)]
    for partner in partners:
        pl.semaphore_signal(barrier, inc=1, device_id=partner, device_id_type=MESH)
    pl.semaphore_wait(barrier, len(partners))

    moved_tables = [
        send(table_ref, tables.at[i], device) for i, device in enumerate(side_devices)
    ]

    half = stored_ref.shape[0] // 2
    moving = {}

    def ring_step(q, step):
        for side in range(2):
            for part in range(2):
                if step == ZS // 2 and side != part:
                    continue
                if step == 1:
                    if side == 0 and part == 0:
                        own_stored[q].wait()
                else:
                    moving[(q, step - 1, side, part)].wait_recv()
                owner = (z + (ZS - step + 1 if side == 0 else step - 1)) % ZS
                block = gathered[q].at[owner, pl.ds(part * half, half)]
                moving[(q, step, side, part)] = send(block, block, right if side == 0 else left)

    def pick(q):
        for side in range(2):
            for part in range(2):
                if side == part:
                    moving[(q, ZS // 2, side, part)].wait_recv()
                else:
                    moving[(q, ZS // 2 - 1, side, part)].wait_recv()
        if q == 0:
            own_table.wait()
            for i, copy in enumerate(moved_tables):
                copy.wait_recv()
            copies = [local(tables.at[i], table_smem.at[i + 1]) for i in range(len(sides))]
            for copy in copies:
                copy.wait()
        for i in range(len(sides) + 1):
            for z_ in range(ZS):
                block = table_smem[i, 0, h * (2 * ZS) + z_ * 2 + c]
                value = gathered[q][z_, block]
                if i == 0:
                    slots[q][h * 2 + c, z_] = value
                else:
                    picked[q][i - 1, z_] = value
        moving[(q, "slots")] = [
            send(picked[q].at[i], slots[q].at[h * 2 + c], device)
            for i, device in enumerate(side_devices)
        ]

    def sort(q):
        for copy in moving[(q, "slots")]:
            copy.wait_recv()
        count = CHUNKS[q]
        for r in range(2 * spans):
            source = ids_ref[r] // 8
            side = (source // (2 * ZS)) * 2 + source % 2
            sorted_[q][r // (2 * mine), r % (2 * mine)] = slots[q][side, (source // 2) % ZS]
        place = pl.ds(pl.multiple_of(t * count, 16), count)
        moving[(q, "sorted")] = [
            send(sorted_[q].at[x_of[d]], features[q].at[:, place, :], at_tp(x_of[d], (l + e) % 2))
            for d in range(XS)
            for e in range(2)
            if (d, e) != (0, 0)
        ]
        moving[(q, "own")] = local(sorted_[q].at[x], features[q].at[:, place, :])

    weight_half = weights.shape[1] // 2
    quarter = weight_half // 2
    own_rows = pl.ds(pl.multiple_of(c * weight_half, 16), weight_half)

    def begin_side_work():
        own_weight.wait()
        part = weights.at[x, own_rows]
        moving["w+"] = send(part, part, at_tp(x_of[1], l))
        moving["w-"] = send(part, part, at_tp(x_of[3], l))
        rows = 2 * mine * SPAN // 2
        for d in range(1, XS):
            start = pl.multiple_of(x_of[d] * rows, 16)
            moving[("q", d)] = send(window_ref.at[pl.ds(start, rows)], queries.at[x], at_tp(x_of[d], l))
        start = pl.multiple_of(x * rows, 16)
        moving[("q", 0)] = local(window_ref.at[pl.ds(start, rows)], queries.at[x])

    def forward_weights():
        for key, to, frm, k in (("w+", 1, 3, 0), ("w-", 3, 1, 1)):
            moving[key].wait_recv()
            rows = pl.ds(pl.multiple_of(c * weight_half + k * quarter, 16), quarter)
            part = weights.at[x_of[frm], rows]
            moving[key + "far"] = send(part, part, at_tp(x_of[to], l))
            part = weights.at[x_of[frm], own_rows]
            moving[key + "core"] = send(part, part, other_core)

    def finish_weights():
        for key in ("w+", "w-"):
            moving[key + "far"].wait_recv()
        part = weights.at[x_of[2], own_rows]
        moving["wfarcore"] = send(part, part, other_core)

    what_ran = 0
    for what in ring_events(n):
        if what[0] == "ring":
            ring_step(what[1], what[2])
        elif what[0] == "pick":
            pick(what[1])
        else:
            sort(what[1])
        what_ran += 1
        if what_ran == 1:
            begin_side_work()
        if what == ("pick", 0):
            forward_weights()
        if what == ("pick", n - 1):
            finish_weights()

    for d in range(XS):
        moving[("q", d)].wait() if d == 0 else moving[("q", d)].wait_recv()
    for key in ("w+core", "w-core", "wfarcore"):
        moving[key].wait_recv()
    for q in range(n):
        moving[(q, "own")].wait()
        for copy in moving[(q, "sorted")]:
            copy.wait_recv()

    def back(u, d):
        rows = pl.ds(pl.multiple_of((x * mine + u) * SPAN, SPAN), SPAN)
        return pltpu.make_async_remote_copy(
            src_ref=results.at[u, d],
            dst_ref=out_ref.at[rows],
            send_sem=back_send.at[u, d - 1],
            recv_sem=back_recv.at[u, d - 1],
            device_id=at_tp(x_of[d], l),
            device_id_type=MESH,
        )

    def span_step(u, carry):
        pair = [
            jnp.concatenate([features[q][2 * u], features[q][2 * u + 1]], axis=1) for q in range(n)
        ]
        for d in (2, 1, 3, 0):
            first = 0
            parts = []
            for q in range(n):
                parts.append(weights[x_of[d], :, first : first + 8 * CHUNKS[q]])
                first += 8 * CHUNKS[q]
            rows = queries[x_of[d], pl.ds(pl.multiple_of(u * SPAN, SPAN), SPAN)]
            value = heads_of_span(parts, pair, rows, head_count)
            if d == 0:
                out_ref[pl.ds(pl.multiple_of((x * mine + u) * SPAN, SPAN), SPAN)] = value
            else:
                results[u, d] = value
                back(u, d).start()
        return carry

    lax.fori_loop(0, mine, span_step, 0)

    for copy in sent:
        copy.wait_send()
    for u in range(mine):
        for d in range(1, XS):
            back(u, d).wait()


def shards(queries, neighbours, key_weight, value_weight, neighbour_ids):
    tok_rows, columns = queries.shape
    span_count = neighbour_ids.shape[0]
    seq_count = lax.axis_size("seq")
    blocks, depth, length = neighbours.shape
    tps = lax.axis_size("tp")
    edge_rows = SPAN - 1
    incoming = passed_along(queries[:edge_rows], "seq", -1)
    windows = jnp.concatenate([queries[edge_rows:], incoming], axis=0)
    weights = jnp.concatenate([key_weight, value_weight], axis=1).T.reshape(2 * columns, tps, depth)
    first, parts = 0, []
    for count in CHUNKS:
        parts.append(weights[:, :, first : first + count].reshape(2 * columns, tps * count))
        first += count
    weights = jnp.concatenate(parts, axis=1)
    ids = neighbour_ids.reshape(-1)
    wanted = (ids // blocks)[None, :] == jnp.arange(seq_count)[:, None]
    table = jnp.sum(jnp.where(wanted, (ids % blocks)[None, :], 0), axis=1)
    table = jnp.zeros((8, 128), jnp.int32).at[0, :seq_count].set(table)
    n = len(CHUNKS)
    bf16 = jnp.bfloat16
    mine = span_count // XS
    scratch = [pltpu.VMEM((ZS, blocks, r, length), bf16) for r in CHUNKS]
    scratch += [pltpu.VMEM((3, ZS, r, length), bf16) for r in CHUNKS]
    scratch += [pltpu.VMEM((4, ZS, r, length), bf16) for r in CHUNKS]
    scratch += [pltpu.VMEM((XS, 2 * mine, r, length), bf16) for r in CHUNKS]
    scratch += [pltpu.VMEM((2 * mine, tps * r, length), bf16) for r in CHUNKS]
    scratch += [
        pltpu.VMEM((XS, 2 * columns, depth * tps), bf16),
        pltpu.VMEM((XS, mine * SPAN, columns), bf16),
        pltpu.VMEM((mine, XS, SPAN, columns), bf16),
        pltpu.VMEM((3, 8, 128), jnp.int32),
        pltpu.SMEM((4, 8, 128), jnp.int32),
        pltpu.SemaphoreType.DMA((160,)),
        pltpu.SemaphoreType.DMA((160,)),
        pltpu.SemaphoreType.DMA((32,)),
        pltpu.SemaphoreType.DMA((mine, XS - 1)),
        pltpu.SemaphoreType.DMA((mine, XS - 1)),
    ]
    blended = pl.pallas_call(
        functools.partial(kernel, n_chunks=n, head_count=columns // HDIM),
        out_shape=jax.ShapeDtypeStruct((tok_rows, columns), bf16),
        in_specs=[
            pl.BlockSpec(memory_space=pltpu.SMEM),
            pl.BlockSpec(memory_space=pltpu.VMEM),
            pl.BlockSpec(memory_space=pl.ANY),
            pl.BlockSpec(memory_space=pl.ANY),
            pl.BlockSpec(memory_space=pltpu.VMEM),
        ],
        out_specs=pl.BlockSpec(memory_space=pltpu.VMEM),
        scratch_shapes=scratch,
        compiler_params=pltpu.CompilerParams(
            collective_id=0, has_side_effects=True, vmem_limit_bytes=50 * 1024 * 1024
        ),
    )(ids, table, neighbours, weights, windows)
    carried = passed_along(blended[tok_rows - edge_rows :], "seq", 1)
    return jnp.concatenate([carried, blended[: tok_rows - edge_rows]], axis=0)


def solution(mesh):
    in_specs = (P("seq", "tp"), P("seq", "tp", None), P(None, "tp"), P(None, "tp"), P("seq", None))
    out_specs = P("seq", "tp")
    return jax.shard_map(shards, mesh=mesh, in_specs=in_specs, out_specs=out_specs, check_vma=False)
```

time: 409 us -> 161 us (0.39)
  waiting for transfers between devices: 342 us -> 1.24 us
  Pallas kernels: 25.3 us -> 134 us
  between operations: 13.5 us -> 0.13 us
  local copies, waits for them, and re-layouts: 13.9 us -> 4.85 us
  starting transfers between devices: 5.94 us -> 12.6 us
    all_gather x2 -> x0, waiting for transfers between devices: 340 us -> none  [the longest x1 196 us: shards(): stored = lax.all_gather(neighbours, 'seq', axis=0, tiled=True)]
    pallas_call x1, Pallas kernels: 25.3 us -> 134 us  [shards(): pl.pallas_call(functools.partial(kernel, n_chunks=n, head_count=columns /...]
    gather x1 -> x0, local copies, waits for them, and re-layouts: 6.79 us -> none  [shards(): chosen = stored[neighbour_ids.reshape(-1)]]
    ppermute x2, starting transfers between devices: 5.89 us -> 12.6 us  [passed_along(): return lax.ppermute(x, axis, pairs)]
    concatenate x0 -> x2, other arithmetic: none -> 4.1 us  [the longest x1 2.45 us: shards(): weights = jnp.concatenate(parts, axis=1)]
  transfers between devices with their start and end apart: 4 -> 2, of which waited for: 3 -> 1; matrix products, arithmetic and copies ran while one was open for 1% -> 4% of each run, Pallas kernels for 0% -> 0%
where the time goes in v2:
time: 161 us; the launch traced here: 158 us
  Pallas kernels  134 us (83%)
  starting transfers between devices  12.6 us (8%)
  other arithmetic  5.48 us (3%)
  local copies, waits for them, and re-layouts  4.85 us (3%)
    pallas_call x1, Pallas kernels, shards(): pl.pallas_call(functools.partial(kernel, n_chunks=n, head_count=columns /...  134 us
    ppermute x2, starting transfers between devices, passed_along(): return lax.ppermute(x, axis, pairs)  12.6 us
  transfers between devices with their start and end apart: 2, of which 1 were waited for; matrix products, arithmetic and copies ran while one was open for 4% of the time, Pallas kernels for 0%

profile of v2, /device:TPU:1, one launch (start us, length us, event | category | flops | bytes accessed | tf_op | source)
XLA Modules:
  0.0 157.8 jit_solution(12069357732490178432)
XLA Ops:
  0.0 0.8 slice.41
  0.8 8.8 %collective-permute-start = (bf16[63,512]{1,0:T(8,128)(2,1)S(1)}, bf16[63,512]{1,0:T(8,128)(2,1)S(1)}, u32[]{:S(2)}, u32[]{:S(2)}) collective-permute-start(bf16[63,512]{1,0:T(8,128)(2,1)S(1)} %slice.41), channel_id=1, source_target_pairs={{8,0},{16,8},{24,16},{32,24},{40,32},{48,40},{56,48},{64,56},{72,6... | collective-permute-start | bytes 193544 | tf_op jit(solution)/shard_map/ppermute | solution.py:22
  9.6 1.7 %pad_maximum_fusion = bf16[896,1024]{1,0:T(8,128)(2,1)S(1)} fusion(bf16[896,512]{1,0:T(8,128)(2,1)} %param.10, bf16[896,512]{1,0:T(8,128)(2,1)} %param.9), kind=kLoop, calls=%fused_computation | loop fusion | flops 3670016 | bytes 3670016 | tf_op jit(solution)/shard_map/concatenate | solution.py:296
  11.3 0.0 copy-start.1
  11.3 0.1 fusion
  11.4 0.1 slice.46
  11.5 1.0 copy-done.1
  12.5 0.2 slice.40
  12.7 0.0 copy-start.2
  12.8 0.2 copy.15
  13.0 1.0 copy.16
  14.0 0.4 copy.17
  14.3 0.0 copy-done.2
  14.3 0.1 copy.14
  14.4 0.1 reshape.94.ids_ref
  14.5 2.4 %pad_maximum_fusion.1.weight_ref = bf16[1024,896]{1,0:T(8,128)(2,1)} fusion(bf16[1024,384]{1,0:T(8,128)(2,1)S(1)} %copy.17, bf16[1024,256]{1,0:T(8,128)(2,1)} %copy.16, bf16[1024,256]{1,0:T(8,128)(2,1)S(1)} %copy.15), kind=kLoop, calls=%fused_computation.1 | loop fusion | flops 5505024 | bytes 3670016 | tf_op jit(solution)/shard_map/concatenate | solution.py:301
  17.0 0.0 copy-start
  17.0 0.1 select_reduce_fusion
  17.1 0.0 collective-permute-done
  17.1 0.1 pad_maximum_fusion.2.window_ref
  17.2 0.7 copy-done
  17.9 133.5 %shard_map.55 = bf16[1024,512]{1,0:T(8,128)(2,1)S(1)} custom-call(s32[32]{0:T(128)S(1)} %reshape.94.ids_ref, s32[8,128]{1,0:T(8,128)S(1)} %scatter.4.table_ref, bf16[8,112,128]{2,1,0:T(8,128)(2,1)S(1)} %copy-done, bf16[1024,896]{1,0:T(8,128)(2,1)} %pad_maximum_fusion.1.weight_ref, bf16[1024,512]{1,0:T(8,128)(2,1)S(1)} %pad_maximum_fusion.2.window_ref), custom_call_target="tpu_custom_call" | custom-call | tf_op jit(solution)/shard_map/pallas_call | solution.py:326
  151.5 3.8 %collective-permute-start.1 = (bf16[63,512]{1,0:T(8,128)(2,1)S(1)}, bf16[63,512]{1,0:T(8,128)(2,1)S(1)}, u32[]{:S(2)}, u32[]{:S(2)}) collective-permute-start(bf16[63,512]{1,0:T(8,128)(2,1)S(1)} %slice.42), channel_id=1, source_target_pairs={{0,8},{8,16},{16,24},{24,32},{32,40},{40,48},{48,56},{56,64},{64,7... | collective-permute-start | bytes 193544 | tf_op jit(solution)/shard_map/ppermute | solution.py:22
  155.3 0.1 slice.43
  155.4 1.2 collective-permute-done.1
  156.6 1.2 pad_maximum_fusion.3
  (3 shorter events, 0.0 us)
Async XLA Ops:
  0.8 16.2 %collective-permute-start = (bf16[63,512]{1,0:T(8,128)(2,1)S(1)}, bf16[63,512]{1,0:T(8,128)(2,1)S(1)}, u32[]{:S(2)}, u32[]{:S(2)}) collective-permute-start(bf16[63,512]{1,0:T(8,128)(2,1)S(1)} %slice.41), channel_id=1, source_target_pairs={{8,0},{16,8},{24,16},{32,24},{40,32},{48,40},{56,48},{64,56},{72,6... | collective-permute-start | bytes 193544 | tf_op jit(solution)/shard_map/ppermute | solution.py:22
  11.3 1.2 copy-start.1
  12.7 1.6 %copy-start.2 = (s32[16,2]{0,1:T(2,128)S(1)}, s32[16,2]{0,1:T(2,128)}, u32[]{:S(2)}) copy-start(s32[16,2]{0,1:T(2,128)} %param.11) | copy-start | bytes 388
  17.0 0.9 copy-start
  151.5 5.2 %collective-permute-start.1 = (bf16[63,512]{1,0:T(8,128)(2,1)S(1)}, bf16[63,512]{1,0:T(8,128)(2,1)S(1)}, u32[]{:S(2)}, u32[]{:S(2)}) collective-permute-start(bf16[63,512]{1,0:T(8,128)(2,1)S(1)} %slice.42), channel_id=1, source_target_pairs={{0,8},{8,16},{16,24},{24,32},{32,40},{40,48},{48,56},{56,64},{64,7... | collective-permute-start | bytes 193544 | tf_op jit(solution)/shard_map/ppermute | solution.py:22

commit v3 on v1

v3 whole, which is shorter than its diff:
```python
import functools

import jax
import jax.numpy as jnp
from jax import lax
from jax.experimental import pallas as pl
from jax.experimental.pallas import tpu as pltpu
from jax.sharding import PartitionSpec as P

HDIM = 128
SPAN = 64
ZS = 16
XS = 4
PARTS = 4
MESH = pl.DeviceIdType.MESH


def heads_of_span(rows, queries, head_count):
    columns = head_count * HDIM
    results = []
    for head in range(head_count):
        at = head * HDIM
        scores = jnp.dot(
            queries[:, at : at + HDIM], rows[at : at + HDIM], preferred_element_type=jnp.float32
        ) * (HDIM**-0.5)
        highest = jnp.max(scores, axis=1, keepdims=True)
        exponent = jnp.exp(scores - highest)
        totals = jnp.sum(exponent, axis=1, keepdims=True)
        blended = lax.dot_general(
            exponent.astype(jnp.bfloat16),
            rows[columns + at : columns + at + HDIM],
            (((1,), (1,)), ((), ())),
            preferred_element_type=jnp.float32,
        )
        results.append((blended / totals).astype(jnp.bfloat16))
    return jnp.concatenate(results, axis=1)


def kernel(
    ids_ref, table_ref, stored_ref, key_ref, value_ref, query_ref, out_ref, *scratch, head_count
):
    gathered = scratch[:ZS]
    (picked, slots, sorted_, features, raw_weights, weights, own_queries, queries, results, blended,
     tables, table_smem, send_sems, recv_sems, local_sems, back_send, back_recv) = scratch[ZS:]
    s, t = lax.axis_index("seq"), lax.axis_index("tp")
    seqs = lax.axis_size("seq")
    h, z, c = s // (2 * ZS), (s // 2) % ZS, s % 2
    x, l = t // 2, t % 2
    columns = head_count * HDIM
    tokens = out_ref.shape[0]
    spans = tokens // SPAN
    mine = spans // XS
    counter = [0, 0]
    sent = []

    def at_tp(x_, l_):
        return (s, x_ * 2 + l_)

    def send(src, dst, device):
        i = counter[0]
        counter[0] += 1
        copy = pltpu.make_async_remote_copy(
            src_ref=src,
            dst_ref=dst,
            send_sem=send_sems.at[i],
            recv_sem=recv_sems.at[i],
            device_id=device,
            device_id_type=MESH,
        )
        copy.start()
        sent.append(copy)
        return copy

    def local(src, dst):
        i = counter[1]
        counter[1] += 1
        copy = pltpu.make_async_copy(src, dst, local_sems.at[i])
        copy.start()
        return copy

    right = (h * (2 * ZS) + (z + 1) % ZS * 2 + c, t)
    left = (h * (2 * ZS) + (z + ZS - 1) % ZS * 2 + c, t)
    after, before = ((s + 1) % seqs, t), ((s + seqs - 1) % seqs, t)
    sides = [(0, 1), (1, 0), (1, 1)]
    side_devices = [
        (((h + a) % 2) * (2 * ZS) + z * 2 + (c + b) % 2, x * 2 + (l + a) % 2) for a, b in sides
    ]
    other_core = side_devices[0]
    x_of = [(x + d) % XS for d in range(XS)]

    own_stored = local(stored_ref, gathered[0])
    own_table = local(table_ref, table_smem.at[0])
    own_raw = [local(key_ref, raw_weights.at[0]), local(value_ref, raw_weights.at[1])]
    own_rows_in = local(query_ref, own_queries.at[pl.ds(0, tokens)])

    barrier = pltpu.get_barrier_semaphore()
    partners = [right, left, after, before] + side_devices
    partners += [at_tp(x_of[d], l) for d in range(1, XS)] + [at_tp(x, 1 - l)]
    for partner in partners:
        pl.semaphore_signal(barrier, inc=1, device_id=partner, device_id_type=MESH)
    pl.semaphore_wait(barrier, len(partners))

    size = stored_ref.shape[0] // PARTS
    ring = {}

    def ring_step(step):
        for part in range(PARTS):
            for side in range(2):
                if step > 1:
                    ring[(step - 1, side, part)].wait_recv()
                if step == ZS // 2 and side != part // (PARTS // 2):
                    continue
                sign = 1 if side == 0 else -1
                blocks = pl.ds(part * size, size)
                ring[(step, side, part)] = send(
                    gathered[sign * (step - 1)].at[blocks],
                    gathered[(sign * step) % ZS].at[blocks],
                    right if side == 0 else left,
                )

    def ring_end():
        for part in range(PARTS):
            ring[(ZS // 2, part // (PARTS // 2), part)].wait_recv()

    slot_copies = []

    def pick(k):
        z_ = (z + (ZS - k)) % ZS
        place = h * (2 * ZS) + z_ * 2 + c
        for i in range(len(sides) + 1):
            value = gathered[k % ZS][table_smem[i, 0, place]]
            if i == 0:
                slots[c, z_] = value
            else:
                picked[i - 1, k % ZS] = value
                slot_copies.append(
                    send(
                        picked.at[i - 1, k % ZS],
                        slots.at[2 * sides[i - 1][0] + c, z_],
                        side_devices[i - 1],
                    )
                )

    side_work = {}
    weight_rows = weights.shape[1] // 2
    quarter = weight_rows // 2
    own_half = pl.ds(pl.multiple_of(c * weight_rows, weight_rows), weight_rows)

    def transpose_weights():
        for copy in own_raw:
            copy.wait()
        for k in range(raw_weights.shape[1] // HDIM):
            part = pl.ds(k * HDIM, HDIM)
            weights[x, own_half, part] = raw_weights[c, part].T
        part = weights.at[x, own_half]
        side_work["w+"] = send(part, part, at_tp(x_of[1], l))
        side_work["w-"] = send(part, part, at_tp(x_of[3], l))
        side_work["core"] = [send(part, part, other_core)]

    def forward_weights():
        for key, to, frm, k in (("w+", 1, 3, 0), ("w-", 3, 1, 1)):
            side_work[key].wait_recv()
            rows = pl.ds(pl.multiple_of(c * weight_rows + k * quarter, quarter), quarter)
            part = weights.at[x_of[frm], rows]
            side_work[key + "far"] = send(part, part, at_tp(x_of[to], l))
            part = weights.at[x_of[frm], own_half]
            side_work["core"].append(send(part, part, other_core))

    def finish_weights():
        for key in ("w+far", "w-far"):
            side_work[key].wait_recv()
        part = weights.at[x_of[2], own_half]
        side_work["core"].append(send(part, part, other_core))

    def send_edge():
        own_rows_in.wait()
        side_work["edge"] = send(
            own_queries.at[pl.ds(0, SPAN)], own_queries.at[pl.ds(tokens, SPAN)], before
        )

    window = queries.shape[1]

    def send_queries():
        side_work["edge"].wait_recv()
        side_work["q"] = []
        for d in range(XS):
            start = pl.multiple_of(x_of[d] * (mine * SPAN) + SPAN - 16, 16)
            src, dst = own_queries.at[pl.ds(start, window)], queries.at[x]
            side_work["q"].append(local(src, dst) if d == 0 else send(src, dst, at_tp(x_of[d], l)))

    own_stored.wait()
    moved_tables = [
        send(table_ref, tables.at[i], device) for i, device in enumerate(side_devices)
    ]
    for step in range(1, ZS // 2 + 1):
        ring_step(step)
        if step == 1:
            send_edge()
            transpose_weights()
        elif step == 2:
            own_table.wait()
            for copy in moved_tables:
                copy.wait_recv()
            copies = [local(tables.at[i], table_smem.at[i + 1]) for i in range(len(sides))]
            for copy in copies:
                copy.wait()
            pick(0)
            send_queries()
        if step > 1:
            pick(step - 1)
            pick(1 - step)
        if step == 5:
            forward_weights()
        if step == 8:
            finish_weights()
    ring_end()
    pick(ZS // 2)

    order = [(i + mine - 1) % mine for i in range(mine)]
    to_handlers, across = {}, {}

    def handler_copy(u, d):
        return send(sorted_.at[x_of[d], u], features.at[u, :, t], at_tp(x_of[d], l))

    def across_copy(u, d):
        part = features.at[u, :, x_of[d] * 2 + l]
        return send(part, part, at_tp(x, 1 - l))

    for copy in slot_copies:
        copy.wait_recv()
    for u in order:
        for x_ in range(XS):
            for j in range(2):
                source = ids_ref[(x_ * mine + u) * 2 + j] // 8
                side = ((source // (2 * ZS) + h) % 2) * 2 + source % 2
                sorted_[x_, u, j] = slots[side, (source // 2) % ZS]
        for d in (2, 1, 3):
            to_handlers[(u, d)] = handler_copy(u, d)
        features[u, :, t] = sorted_[x, u]
        across[(u, 0)] = across_copy(u, 0)
    for u in order:
        for d in (3, 1, 2):
            to_handlers[(u, d)].wait_recv()
            across[(u, d)] = across_copy(u, (XS - d) % XS)

    for i in range(XS):
        side_work["q"][i].wait() if i == 0 else side_work["q"][i].wait_recv()
    for copy in side_work["core"]:
        copy.wait_recv()

    def result_rows(span):
        return pl.ds(pl.multiple_of((span + 1) * SPAN, SPAN), SPAN)

    def back(u, d):
        return pltpu.make_async_remote_copy(
            src_ref=results.at[u, d],
            dst_ref=blended.at[result_rows(x * mine + u)],
            send_sem=back_send.at[u, d - 1],
            recv_sem=back_recv.at[u, d - 1],
            device_id=at_tp(x_of[d], l),
            device_id_type=MESH,
        )

    def features_of(u, j):
        source = ids_ref[(x * mine + u) * 2 + j] // 8
        other = (source // (2 * ZS) + h) % 2 == 1
        parts = []
        for k in range(XS):
            low, high = features[u, j, 2 * k], features[u, j, 2 * k + 1]
            parts += [jnp.where(other, high, low), jnp.where(other, low, high)]
        return jnp.concatenate(parts, axis=0)

    for i, u in enumerate(order):
        for d in range(XS):
            across[(u, d)].wait_recv()
        pair = jnp.concatenate([features_of(u, 0), features_of(u, 1)], axis=1)
        for d in (2, 1, 3, 0):
            rows = jnp.dot(weights[x_of[d]], pair, preferred_element_type=jnp.float32)
            wanted = queries[x_of[d], pl.ds(u * SPAN, SPAN + 16)].astype(jnp.float32)
            wanted = wanted[15 : 15 + SPAN].astype(jnp.bfloat16)
            value = heads_of_span(rows.astype(jnp.bfloat16), wanted, head_count)
            if d == 0:
                blended[result_rows(x * mine + u)] = value
            else:
                results[u, d] = value
                back(u, d).start()
        if i == 1:
            for d in range(1, XS):
                back(order[0], d).wait_recv()
            carried = send(blended.at[pl.ds(tokens, SPAN)], blended.at[pl.ds(0, SPAN)], after)

    for u in order[1:]:
        for d in range(1, XS):
            back(u, d).wait_recv()
    carried.wait_recv()
    for i in range(spans):
        rows = blended[pl.ds(i * SPAN, SPAN + 16)].astype(jnp.float32)[1 : 1 + SPAN]
        if i == 0:
            places = lax.broadcasted_iota(jnp.int32, rows.shape, 0)
            rows = jnp.where((s == 0) & (places < SPAN - 1), 0.0, rows)
        out_ref[pl.ds(i * SPAN, SPAN)] = rows.astype(jnp.bfloat16)
    for copy in sent:
        copy.wait_send()
    for u in order:
        for d in range(1, XS):
            back(u, d).wait_send()


def shards(queries, neighbours, key_weight, value_weight, neighbour_ids):
    tok_rows, columns = queries.shape
    span_count = neighbour_ids.shape[0]
    blocks, depth, length = neighbours.shape
    tps = lax.axis_size("tp")
    ids = neighbour_ids.reshape(-1)
    wanted = (ids // blocks)[None, :] == jnp.arange(1024)[:, None]
    table = jnp.sum(jnp.where(wanted, (ids % blocks)[None, :], 0), axis=1).reshape(8, 128)
    bf16 = jnp.bfloat16
    mine = span_count // XS
    scratch = [pltpu.VMEM((blocks, depth, length), bf16) for _ in range(ZS)]
    scratch += [
        pltpu.VMEM((3, ZS, depth, length), bf16),
        pltpu.VMEM((4, ZS, depth, length), bf16),
        pltpu.VMEM((XS, mine, 2, depth, length), bf16),
        pltpu.VMEM((mine, 2, tps, depth, length), bf16),
        pltpu.VMEM((2, depth * tps, columns), bf16),
        pltpu.VMEM((XS, 2 * columns, depth * tps), bf16),
        pltpu.VMEM((tok_rows + SPAN, columns), bf16),
        pltpu.VMEM((XS, mine * SPAN + 16, columns), bf16),
        pltpu.VMEM((mine, XS, SPAN, columns), bf16),
        pltpu.VMEM((tok_rows + SPAN, columns), bf16),
        pltpu.VMEM((3, 8, 128), jnp.int32),
        pltpu.SMEM((4, 8, 128), jnp.int32),
        pltpu.SemaphoreType.DMA((192,)),
        pltpu.SemaphoreType.DMA((192,)),
        pltpu.SemaphoreType.DMA((16,)),
        pltpu.SemaphoreType.DMA((mine, XS - 1)),
        pltpu.SemaphoreType.DMA((mine, XS - 1)),
    ]
    return pl.pallas_call(
        functools.partial(kernel, head_count=columns // HDIM),
        out_shape=jax.ShapeDtypeStruct((tok_rows, columns), bf16),
        in_specs=[
            pl.BlockSpec(memory_space=pltpu.SMEM),
            pl.BlockSpec(memory_space=pltpu.VMEM),
            pl.BlockSpec(memory_space=pl.ANY),
            pl.BlockSpec(memory_space=pl.ANY),
            pl.BlockSpec(memory_space=pl.ANY),
            pl.BlockSpec(memory_space=pl.ANY),
        ],
        out_specs=pl.BlockSpec(memory_space=pltpu.VMEM),
        scratch_shapes=scratch,
        compiler_params=pltpu.CompilerParams(
            collective_id=0, has_side_effects=True, vmem_limit_bytes=50 * 1024 * 1024
        ),
    )(ids, table, neighbours, key_weight, value_weight, queries)


def solution(mesh):
    in_specs = (P("seq", "tp"), P("seq", "tp", None), P(None, "tp"), P(None, "tp"), P("seq", None))
    out_specs = P("seq", "tp")
    return jax.shard_map(shards, mesh=mesh, in_specs=in_specs, out_specs=out_specs, check_vma=False)
```

time: 409 us -> 116 us (0.28); the launches traced: 404 us -> 116 us
  waiting for transfers between devices: 342 us -> 0 us
  Pallas kernels: 25.3 us -> 111 us
  between operations: 13.5 us -> 0.04 us
  local copies, waits for them, and re-layouts: 13.9 us -> 5.1 us
  starting transfers between devices: 5.94 us -> 0 us
    all_gather x2 -> x0, waiting for transfers between devices: 340 us -> none  [the longest x1 196 us: shards(): stored = lax.all_gather(neighbours, 'seq', axis=0, tiled=True)]
    pallas_call x1, Pallas kernels: 25.3 us -> 111 us  [shards(): pl.pallas_call(functools.partial(kernel, head_count=columns // HDIM), out...]
    gather x1 -> x0, local copies, waits for them, and re-layouts: 6.79 us -> none  [shards(): chosen = stored[neighbour_ids.reshape(-1)]]
    ppermute x2 -> x0, starting transfers between devices: 5.89 us -> none  [passed_along(): return lax.ppermute(x, axis, pairs)]
  transfers between devices with their start and end apart: 4 -> 0, of which waited for: 3 -> 0; matrix products, arithmetic and copies ran while one was open for 1% -> 0% of each run, Pallas kernels for 0% -> 0%
where the time goes in v3:
time: 116 us
  Pallas kernels  111 us (96%)
  local copies, waits for them, and re-layouts  5.1 us (4%)
    pallas_call x1, Pallas kernels, shards(): pl.pallas_call(functools.partial(kernel, head_count=columns // HDIM), out...  111 us
    unnamed x8, local copies, waits for them, and re-layouts  5.02 us

profile of v3, /device:TPU:1, one launch (start us, length us, event | category | flops | bytes accessed | tf_op | source)
XLA Modules:
  0.0 116.0 jit_solution(12082970643948618729)
XLA Ops:
  0.0 0.8 copy.8
  0.8 0.1 reshape.55.ids_ref
  0.9 0.1 select_reduce_fusion
  1.0 0.0 copy-start
  1.0 1.2 %copy-done = bf16[896,512]{1,0:T(8,128)(2,1)S(1)} copy-done((bf16[896,512]{1,0:T(8,128)(2,1)S(1)}, bf16[896,512]{1,0:T(8,128)(2,1)}, u32[]{:S(2)}) %copy-start) | copy-done | bytes 917528
  2.1 0.0 copy-start.1
  2.1 1.2 %copy-done.1 = bf16[896,512]{1,0:T(8,128)(2,1)S(1)} copy-done((bf16[896,512]{1,0:T(8,128)(2,1)S(1)}, bf16[896,512]{1,0:T(8,128)(2,1)}, u32[]{:S(2)}) %copy-start.1) | copy-done | bytes 917528
  3.3 0.0 copy-start.2
  3.3 0.9 copy-done.2
  4.3 110.8 %shard_map.55 = bf16[1024,512]{1,0:T(8,128)(2,1)S(1)} custom-call(s32[32]{0:T(128)S(1)} %reshape.55.ids_ref, s32[8,128]{1,0:T(8,128)S(1)} %bitcast.1, bf16[8,112,128]{2,1,0:T(8,128)(2,1)S(1)} %copy-done.2, bf16[896,512]{1,0:T(8,128)(2,1)S(1)} %copy-done, bf16[896,512]{1,0:T(8,128)(2,1)S(1)} %copy-done.1, bf16[1024,512]{1,0:T(8,128)(2,1)} %query_ref.1), custom_call_target="tpu_custom_call" | custom-call | tf_op jit(solution)/shard_map/pallas_call | solution.py:339
  115.1 1.0 copy.10
  (1 shorter events, 0.0 us)
Async XLA Ops:
  1.0 1.2 %copy-start = (bf16[896,512]{1,0:T(8,128)(2,1)S(1)}, bf16[896,512]{1,0:T(8,128)(2,1)}, u32[]{:S(2)}) copy-start(bf16[896,512]{1,0:T(8,128)(2,1)} %key_ref.1) | copy-start | bytes 2752516
  2.1 1.2 %copy-start.1 = (bf16[896,512]{1,0:T(8,128)(2,1)S(1)}, bf16[896,512]{1,0:T(8,128)(2,1)}, u32[]{:S(2)}) copy-start(bf16[896,512]{1,0:T(8,128)(2,1)} %value_ref.1) | copy-start | bytes 2752516
  3.3 0.9 copy-start.2

commit v4 on v3

--- a/solution.py
+++ b/solution.py
@@ -12,6 +12,8 @@
 ZS = 16
 XS = 4
 PARTS = 4
+GROUPS = ((2, 1), (3, 0))
+FIRST = 1
 MESH = pl.DeviceIdType.MESH
 
 
@@ -237,8 +239,11 @@
         for d in (2, 1, 3):
             to_handlers[(u, d)] = handler_copy(u, d)
         features[u, :, t] = sorted_[x, u]
-        across[(u, 0)] = across_copy(u, 0)
+        if u in order[:FIRST]:
+            across[(u, 0)] = across_copy(u, 0)
     for u in order:
+        if u not in order[:FIRST]:
+            across[(u, 0)] = across_copy(u, 0)
         for d in (3, 1, 2):
             to_handlers[(u, d)].wait_recv()
             across[(u, d)] = across_copy(u, (XS - d) % XS)
@@ -274,16 +279,24 @@
         for d in range(XS):
             across[(u, d)].wait_recv()
         pair = jnp.concatenate([features_of(u, 0), features_of(u, 1)], axis=1)
-        for d in (2, 1, 3, 0):
-            rows = jnp.dot(weights[x_of[d]], pair, preferred_element_type=jnp.float32)
-            wanted = queries[x_of[d], pl.ds(u * SPAN, SPAN + 16)].astype(jnp.float32)
-            wanted = wanted[15 : 15 + SPAN].astype(jnp.bfloat16)
-            value = heads_of_span(rows.astype(jnp.bfloat16), wanted, head_count)
-            if d == 0:
-                blended[result_rows(x * mine + u)] = value
-            else:
-                results[u, d] = value
-                back(u, d).start()
+        for group in GROUPS:
+            projected = {
+                d: jnp.dot(weights[x_of[d]], pair, preferred_element_type=jnp.float32).astype(
+                    jnp.bfloat16
+                )
+                for d in group
+            }
+            for d in group:
+                wanted = queries[x_of[d], pl.ds(u * SPAN, SPAN + 16)].astype(jnp.float32)
+                wanted = wanted[15 : 15 + SPAN].astype(jnp.bfloat16)
+                value = heads_of_span(projected[d], wanted, head_count)
+                if d == 0:
+                    blended[result_rows(x * mine + u)] = value
+                else:
+                    results[u, d] = value
+            for d in group:
+                if d > 0:
+                    back(u, d).start()
         if i == 1:
             for d in range(1, XS):
                 back(order[0], d).wait_recv()
@@ -350,7 +363,7 @@
         out_specs=pl.BlockSpec(memory_space=pltpu.VMEM),
         scratch_shapes=scratch,
         compiler_params=pltpu.CompilerParams(
-            collective_id=0, has_side_effects=True, vmem_limit_bytes=50 * 1024 * 1024
+            collective_id=0, has_side_effects=True, vmem_limit_bytes=63 * 1024 * 1024
         ),
     )(ids, table, neighbours, key_weight, value_weight, queries)
 

time: 116 us -> 104 us (0.90)
  Pallas kernels: 111 us -> 99.1 us
  local copies, waits for them, and re-layouts: 5.1 us -> 3.67 us
    pallas_call x1, Pallas kernels: 111 us -> 99.1 us  [shards(): pl.pallas_call(functools.partial(kernel, head_count=columns // HDIM), out...]
    unnamed x8 -> x4, local copies, waits for them, and re-layouts: 5.02 us -> 3.58 us
where the time goes in v4:
time: 104 us
  Pallas kernels  99.1 us (95%)
  local copies, waits for them, and re-layouts  3.67 us (4%)
    pallas_call x1, Pallas kernels, shards(): pl.pallas_call(functools.partial(kernel, head_count=columns // HDIM), out...  99.1 us
    unnamed x4, local copies, waits for them, and re-layouts  3.58 us

profile of v4, /device:TPU:1, one launch (start us, length us, event | category | flops | bytes accessed | tf_op | source)
XLA Modules:
  0.0 103.5 jit_solution(12563060261298789475)
XLA Ops:
  0.0 0.8 copy.8
  0.8 0.1 reshape.55.ids_ref
  0.8 0.0 copy-start
  0.9 0.6 copy-done
  1.4 0.7 select_reduce_fusion
  2.1 99.1 %shard_map.55 = bf16[1024,512]{1,0:T(8,128)(2,1)} custom-call(s32[32]{0:T(128)} %copy-done, s32[8,128]{1,0:T(8,128)} %bitcast.1, bf16[8,112,128]{2,1,0:T(8,128)(2,1)} %stored_ref.1, bf16[896,512]{1,0:T(8,128)(2,1)} %key_ref.1, bf16[896,512]{1,0:T(8,128)(2,1)} %value_ref.1, bf16[1024,512]{1,0:T(8,128)(2,1)} %query_ref.1), custom_call_target="tpu_custom_call" | custom-call | tf_op jit(solution)/shard_map/pallas_call | solution.py:352
  101.2 2.3 %copy.10 = bf16[1024,512]{1,0:T(8,128)(2,1)} copy(bf16[1024,512]{1,0:T(8,128)(2,1)} %shard_map.55) | data formatting | bytes 2097152
  (1 shorter events, 0.0 us)
Async XLA Ops:
  0.8 0.6 copy-start

commit v5 on v4

--- a/solution.py
+++ b/solution.py
@@ -14,6 +14,11 @@
 PARTS = 4
 GROUPS = ((2, 1), (3, 0))
 FIRST = 1
+AHEAD = 3
+LATE = True
+EARLY_OUT = True
+WEIGHTS_AT = (4, 6)
+QUERIES_AT = 6
 MESH = pl.DeviceIdType.MESH
 
 
@@ -119,12 +124,27 @@
                     gathered[(sign * step) % ZS].at[blocks],
                     right if side == 0 else left,
                 )
+            if LATE:
+                pick_waiting()
+        if step == 2:
+            waiting.append(0)
+        if step > 1:
+            waiting.extend([step - 1, 1 - step])
+        while waiting and not LATE:
+            pick_waiting()
 
     def ring_end():
+        while waiting:
+            pick_waiting()
         for part in range(PARTS):
             ring[(ZS // 2, part // (PARTS // 2), part)].wait_recv()
 
     slot_copies = []
+    waiting = []
+
+    def pick_waiting():
+        if waiting:
+            pick(waiting.pop(0))
 
     def pick(k):
         z_ = (z + (ZS - k)) % ZS
@@ -195,26 +215,23 @@
         send(table_ref, tables.at[i], device) for i, device in enumerate(side_devices)
     ]
     for step in range(1, ZS // 2 + 1):
-        ring_step(step)
-        if step == 1:
-            send_edge()
-            transpose_weights()
-        elif step == 2:
+        if step == 2:
             own_table.wait()
             for copy in moved_tables:
                 copy.wait_recv()
             copies = [local(tables.at[i], table_smem.at[i + 1]) for i in range(len(sides))]
             for copy in copies:
                 copy.wait()
-            pick(0)
+        ring_step(step)
+        if step == 1:
+            send_edge()
+            transpose_weights()
+        if step == WEIGHTS_AT[0]:
+            forward_weights()
+        if step == WEIGHTS_AT[1]:
+            finish_weights()
+        if step == QUERIES_AT:
             send_queries()
-        if step > 1:
-            pick(step - 1)
-            pick(1 - step)
-        if step == 5:
-            forward_weights()
-        if step == 8:
-            finish_weights()
     ring_end()
     pick(ZS // 2)
 
@@ -241,12 +258,16 @@
         features[u, :, t] = sorted_[x, u]
         if u in order[:FIRST]:
             across[(u, 0)] = across_copy(u, 0)
-    for u in order:
+
+    def forward(u):
         if u not in order[:FIRST]:
             across[(u, 0)] = across_copy(u, 0)
         for d in (3, 1, 2):
             to_handlers[(u, d)].wait_recv()
             across[(u, d)] = across_copy(u, (XS - d) % XS)
+
+    for u in order[:AHEAD]:
+        forward(u)
 
     for i in range(XS):
         side_work["q"][i].wait() if i == 0 else side_work["q"][i].wait_recv()
@@ -297,21 +318,31 @@
             for d in group:
                 if d > 0:
                     back(u, d).start()
+        if i + AHEAD < mine:
+            forward(order[i + AHEAD])
         if i == 1:
             for d in range(1, XS):
                 back(order[0], d).wait_recv()
             carried = send(blended.at[pl.ds(tokens, SPAN)], blended.at[pl.ds(0, SPAN)], after)
 
-    for u in order[1:]:
-        for d in range(1, XS):
-            back(u, d).wait_recv()
-    carried.wait_recv()
-    for i in range(spans):
+    def shift_out(i):
         rows = blended[pl.ds(i * SPAN, SPAN + 16)].astype(jnp.float32)[1 : 1 + SPAN]
         if i == 0:
             places = lax.broadcasted_iota(jnp.int32, rows.shape, 0)
             rows = jnp.where((s == 0) & (places < SPAN - 1), 0.0, rows)
         out_ref[pl.ds(i * SPAN, SPAN)] = rows.astype(jnp.bfloat16)
+
+    last = [i for i in range(spans) if not EARLY_OUT or order[-1] in (i % mine, (i - 1) % mine)]
+    for u in order[1:]:
+        if u == order[-1]:
+            carried.wait_recv()
+            for i in range(spans):
+                if i not in last:
+                    shift_out(i)
+        for d in range(1, XS):
+            back(u, d).wait_recv()
+    for i in last:
+        shift_out(i)
     for copy in sent:
         copy.wait_send()
     for u in order:
@@ -355,10 +386,10 @@
         in_specs=[
             pl.BlockSpec(memory_space=pltpu.SMEM),
             pl.BlockSpec(memory_space=pltpu.VMEM),
-            pl.BlockSpec(memory_space=pl.ANY),
-            pl.BlockSpec(memory_space=pl.ANY),
-            pl.BlockSpec(memory_space=pl.ANY),
-            pl.BlockSpec(memory_space=pl.ANY),
+            pl.BlockSpec(memory_space=pltpu.HBM),
+            pl.BlockSpec(memory_space=pltpu.HBM),
+            pl.BlockSpec(memory_space=pltpu.HBM),
+            pl.BlockSpec(memory_space=pltpu.HBM),
         ],
         out_specs=pl.BlockSpec(memory_space=pltpu.VMEM),
         scratch_shapes=scratch,

time: 104 us -> 102 us (0.981)
  the two profiles are of different devices: /device:TPU:1 before, /device:TPU:4 now
where the time goes in v5:
time: 102 us
  Pallas kernels  97.4 us (95%)
  local copies, waits for them, and re-layouts  3.67 us (4%)
    pallas_call x1, Pallas kernels, shards(): pl.pallas_call(functools.partial(kernel, head_count=columns // HDIM), out...  97.4 us
    unnamed x4, local copies, waits for them, and re-layouts  3.58 us

profile of v5, /device:TPU:4, one launch (start us, length us, event | category | flops | bytes accessed | tf_op | source)
XLA Modules:
  0.0 101.8 jit_solution(9101016269923400641)
XLA Ops:
  0.0 0.8 copy.8
  0.8 0.1 reshape.55.ids_ref
  0.8 0.0 copy-start
  0.9 0.6 copy-done
  1.4 0.7 select_reduce_fusion
  2.1 97.4 %shard_map.55 = bf16[1024,512]{1,0:T(8,128)(2,1)} custom-call(s32[32]{0:T(128)} %copy-done, s32[8,128]{1,0:T(8,128)} %bitcast.1, bf16[8,112,128]{2,1,0:T(8,128)(2,1)} %stored_ref.1, bf16[896,512]{1,0:T(8,128)(2,1)} %key_ref.1, bf16[896,512]{1,0:T(8,128)(2,1)} %value_ref.1, bf16[1024,512]{1,0:T(8,128)(2,1)} %query_ref.1), custom_call_target="tpu_custom_call" | custom-call | tf_op jit(solution)/shard_map/pallas_call | solution.py:383
  99.6 2.3 %copy.10 = bf16[1024,512]{1,0:T(8,128)(2,1)} copy(bf16[1024,512]{1,0:T(8,128)(2,1)} %shard_map.55) | data formatting | bytes 2097152
  (1 shorter events, 0.0 us)
Async XLA Ops:
  0.8 0.6 copy-start

commit v6 on v5

--- a/solution.py
+++ b/solution.py
@@ -18,7 +18,7 @@
 LATE = True
 EARLY_OUT = True
 WEIGHTS_AT = (4, 6)
-QUERIES_AT = 6
+QUERIES_AT = 8
 MESH = pl.DeviceIdType.MESH
 
 

time: 102 us -> 108 us (1.059)
  the two profiles are of different devices: /device:TPU:4 before, /device:TPU:14 now
where the time goes in v6:
time: 108 us
  Pallas kernels  104 us (96%)
  local copies, waits for them, and re-layouts  3.67 us (3%)
    pallas_call x1, Pallas kernels, shards(): pl.pallas_call(functools.partial(kernel, head_count=columns // HDIM), out...  104 us
    unnamed x4, local copies, waits for them, and re-layouts  3.58 us

profile of v6, /device:TPU:14, one launch (start us, length us, event | category | flops | bytes accessed | tf_op | source)
XLA Modules:
  0.0 108.3 jit_solution(15079520450897500736)
XLA Ops:
  0.0 0.8 copy.8
  0.8 0.1 reshape.55.ids_ref
  0.8 0.0 copy-start
  0.9 0.6 copy-done
  1.4 0.7 select_reduce_fusion
  2.1 103.9 %shard_map.55 = bf16[1024,512]{1,0:T(8,128)(2,1)} custom-call(s32[32]{0:T(128)} %copy-done, s32[8,128]{1,0:T(8,128)} %bitcast.1, bf16[8,112,128]{2,1,0:T(8,128)(2,1)} %stored_ref.1, bf16[896,512]{1,0:T(8,128)(2,1)} %key_ref.1, bf16[896,512]{1,0:T(8,128)(2,1)} %value_ref.1, bf16[1024,512]{1,0:T(8,128)(2,1)} %query_ref.1), custom_call_target="tpu_custom_call" | custom-call | tf_op jit(solution)/shard_map/pallas_call | solution.py:383
  106.0 2.3 %copy.10 = bf16[1024,512]{1,0:T(8,128)(2,1)} copy(bf16[1024,512]{1,0:T(8,128)(2,1)} %shard_map.55) | data formatting | bytes 2097152
  (1 shorter events, 0.0 us)
Async XLA Ops:
  0.8 0.6 copy-start
